TPU v7x, 32 devices: a whole 2x2x4 slice. The times are simulated.
32 devices in a mesh: chan: 8 (over z, x), win: 4 (over y, core).
Axes of the slice: x: 2, y: 2, z: 4, core: 2. Of those that a mesh axis runs over, the one named last changes fastest.
Arguments:
- spectra: bfloat16 [2, 2, 2048, 4096], P(None, None, 'win', 'chan'), may hold values from -1000 to 1000
- near: int32 [8, 3], P('chan'), may hold values 0 or 1
Outputs:
- cross_spectra: float32 [4096, 4, 2, 2, 512], P(('chan', 'win'))
All inputs are finite; a program needn't handle non-finite values. No bound on the sum of `near` on one device may be relied on, other than what follows from the above.
Results may differ from a plain program's by a relative error of at most 0.014.
Values may be sent and summed in bfloat16 or wider, within the bound.
A program may use at most 64 MiB of HBM per device.

v0:
```python
import jax
import jax.numpy as jnp
from jax import lax
from jax.sharding import PartitionSpec as P

ROUNDS = 3


def shifted(block, axis, distance):
    devices = range(lax.axis_size(axis))
    route = [(i - distance, i) for i in devices if i - distance in devices]
    return lax.ppermute(block, axis, route)


def cross_rows(whitened, partner, start, count, width):
    left_real = lax.dynamic_slice_in_dim(whitened, start, count, 2)
    left_imag = lax.dynamic_slice_in_dim(whitened, width + start, count, 2)
    left = jnp.concatenate([left_real, left_imag], axis=2)
    product = jnp.einsum("fwi,fwj->fij", left, partner, preferred_element_type=jnp.float32)
    real = product[:, :count, :width] + product[:, count:, width:]
    imag = product[:, :count, width:] - product[:, count:, :width]
    return jnp.transpose(jnp.stack([real, imag], axis=0), (2, 0, 1, 3))


def on_device(spectra, near):
    width = spectra.shape[3]
    windows = spectra.shape[2] * lax.axis_size("win")
    real_part = spectra[0].astype(jnp.float32)
    imag_part = spectra[1].astype(jnp.float32)
    power = jnp.sum(real_part * real_part + imag_part * imag_part, axis=1)
    energy = lax.psum(power, "win")
    scale = lax.rsqrt(energy / windows + 1e-06)
    joined = jnp.concatenate([real_part, imag_part], axis=-1)
    whitened = (joined * jnp.concatenate([scale, scale], axis=-1)[:, None, :]).astype(jnp.bfloat16)
    partners = [whitened]
    for step in range(ROUNDS):
        partners.append(shifted(whitened, "chan", step + 1))
    weights = near[0].astype(jnp.float32)
    factors = [jnp.float32(1.0)] + [weights[r] for r in range(ROUNDS)]
    pieces = [
        factors[r] * cross_rows(whitened, partners[r], 0, width, width) for r in range(ROUNDS + 1)
    ]
    summed = lax.psum_scatter(
        jnp.stack(pieces, axis=1).astype(jnp.bfloat16), "win", scatter_dimension=0, tiled=True
    ).astype(jnp.float32)
    return summed * (1.0 / windows)


def solution(mesh):
    return jax.shard_map(
        on_device,
        mesh=mesh,
        in_specs=(P(None, None, "win", "chan"), P("chan", None)),
        out_specs=P(("chan", "win"), None, None, None, None),
        check_vma=False,
    )
```

profile of v0, /device:TPU:16, one launch (start us, length us, event | category | flops | bytes accessed | tf_op | source)
XLA Modules:
  0.0 301.6 jit_solution(9581464129234095386)
XLA Ops:
  6.5 0.0 copy-start
  6.5 0.0 reduce-scatter.2.cloned.1.call-start
  6.5 4.3 %bitcast_convert_fusion.1 = (f32[2,512,512]{2,1,0:T(8,128)}, f32[2,512,512]{2,1,0:T(8,128)}) fusion(bf16[2,2,512,512]{3,2,1,0:T(8,128)(2,1)} %param.2), kind=kLoop, calls=%fused_computation.34 | loop fusion | flops 1048576 | bytes 6291456 | tf_op jit(solution)/shard_map/convert_element_type | solution.py:28
  10.9 0.0 copy-done
  10.9 0.4 add_reduce_fusion
  11.3 6.9 %psum.7 = f32[2,512]{1,0:T(2,128)S(1)} all-reduce(f32[2,512]{1,0:T(2,128)S(1)} %add_reduce_fusion), channel_id=1, replica_groups=mesh['chan'=8,'win'=4] {'win'}, use_global_device_ids=true, to_apply=%region_1.0 | all-reduce | flops 1024 | bytes 8192 | tf_op jit(solution)/shard_map/psum | solution.py:31
  18.2 0.0 copy-start.1
  18.3 2.8 fusion
  21.1 3.5 %collective-permute-start.1 = (bf16[2,512,1024]{2,1,0:T(8,128)(2,1)S(1)}, bf16[2,512,1024]{2,1,0:T(8,128)(2,1)S(1)}, u32[]{:S(2)}, u32[]{:S(2)}) collective-permute-start(bf16[2,512,1024]{2,1,0:T(8,128)(2,1)S(1)} %fusion), channel_id=1, source_target_pairs={{0,8},{4,12},{8,16},{12,20},{16,24},{20,28},{1,9},{5,13},{9,17},{1... | collective-permute-start | bytes 6291464 | tf_op jit(solution)/shard_map/ppermute | solution.py:12
  24.6 2.2 collective-permute-start.2
  26.8 2.7 collective-permute-start
  29.4 0.0 copy-done.1
  29.5 2.5 fusion.18
  31.9 0.8 fusion.15
  32.7 0.7 fusion.17
  33.4 0.2 maximum_bitcast_fusion
  33.6 37.9 %collective-permute-done.1 = bf16[2,512,1024]{2,1,0:T(8,128)(2,1)S(1)} collective-permute-done((bf16[2,512,1024]{2,1,0:T(8,128)(2,1)S(1)}, bf16[2,512,1024]{2,1,0:T(8,128)(2,1)S(1)}, u32[]{:S(2)}, u32[]{:S(2)}) %collective-permute-start.1) | collective-permute-done | bytes 2097184 | tf_op jit(solution)/shard_map/ppermute | solution.py:12
  71.5 2.4 fusion.20
  74.0 1.0 fusion.10
  75.0 42.3 %collective-permute-done.2 = bf16[2,512,1024]{2,1,0:T(8,128)(2,1)S(1)} collective-permute-done((bf16[2,512,1024]{2,1,0:T(8,128)(2,1)S(1)}, bf16[2,512,1024]{2,1,0:T(8,128)(2,1)S(1)}, u32[]{:S(2)}, u32[]{:S(2)}) %collective-permute-start.2) | collective-permute-done | bytes 2097184 | tf_op jit(solution)/shard_map/ppermute | solution.py:12
  117.3 2.4 fusion.21
  119.8 1.0 fusion.8
  120.8 84.1 %collective-permute-done = bf16[2,512,1024]{2,1,0:T(8,128)(2,1)S(1)} collective-permute-done((bf16[2,512,1024]{2,1,0:T(8,128)(2,1)S(1)}, bf16[2,512,1024]{2,1,0:T(8,128)(2,1)S(1)}, u32[]{:S(2)}, u32[]{:S(2)}) %collective-permute-start) | collective-permute-done | bytes 2097184 | tf_op jit(solution)/shard_map/ppermute | solution.py:12
  204.9 2.7 fusion.19
  207.6 1.0 fusion.12
  208.6 1.3 fusion.6
  209.9 2.5 fusion.4
  212.4 3.9 %pad_maximum_fusion = bf16[512,4,2,2,512]{4,0,3,2,1:T(8,128)(2,1)} fusion(bf16[512,1,2,2,512]{4,0,3,2,1:T(8,128)(2,1)S(1)} %get-tuple-element.18, bf16[512,1,2,2,512]{4,0,3,2,1:T(8,128)(2,1)S(1)} %get-tuple-element.19, bf16[512,1,2,2,512]{4,0,3,2,1:T(8,128)(2,1)S(1)} %fusion.6, bf16[512,1,2,2,512]{4,0,3,2,1:T(8,128)(2,1)S(1)} %maximum_bitcast_fusion), kind=kLoop, calls=%fused_computation | loop fusion | flops 12582912 | bytes 16777216 | tf_op jit(solution)/shard_map/stack | solution.py:44
  216.3 0.0 reduce-scatter.2.cloned.1.call-update
  216.3 71.0 %reduce-scatter.2.cloned.1.call-done = bf16[128,4,2,2,512]{4,0,3,2,1:T(8,128)(2,1)} async-done(((bf16[512,4,2,2,512]{4,0,3,2,1:T(8,128)(2,1)}), bf16[128,4,2,2,512]{4,0,3,2,1:T(8,128)(2,1)}) %reduce-scatter.2.cloned.1.call-update) | async-done | bytes 2097168 | tf_op jit(solution)/shard_map/reduce_scatter | solution.py:43
  287.3 2.1 convert_multiply_fusion
  289.5 5.3 %copy.7 = f32[128,4,2,2,512]{4,3,2,1,0:T(2,128)} copy(f32[128,4,2,2,512]{4,0,3,2,1:T(8,128)S(1)} %convert_multiply_fusion) | data formatting | bytes 8388608 | tf_op jit(solution)/shard_map/mul | solution.py:46
  (3 shorter events, 0.0 us)
Async XLA Ops:
  6.5 4.3 %copy-start = (bf16[2,2,512,512]{3,2,1,0:T(8,128)(2,1)S(1)}, bf16[2,2,512,512]{3,2,1,0:T(8,128)(2,1)}, u32[]{:S(2)}) copy-start(bf16[2,2,512,512]{3,2,1,0:T(8,128)(2,1)} %param.2) | copy-start | bytes 6291460
  6.5 280.8 %reduce-scatter.2.cloned.1.call-start = ((), (), s32[]{:S(2)}) async-start(), calls=%async_computation.1 | async-start | bytes 10485760 | tf_op jit(solution)/shard_map/reduce_scatter | solution.py:43
  18.2 11.2 %copy-start.1 = (s32[1,3]{1,0:T(1,128)S(1)}, s32[1,3]{1,0:T(1,128)}, u32[]{:S(2)}) copy-start(s32[1,3]{1,0:T(1,128)} %param.3) | copy-start | bytes 40
  21.1 50.5 %collective-permute-start.1 = (bf16[2,512,1024]{2,1,0:T(8,128)(2,1)S(1)}, bf16[2,512,1024]{2,1,0:T(8,128)(2,1)S(1)}, u32[]{:S(2)}, u32[]{:S(2)}) collective-permute-start(bf16[2,512,1024]{2,1,0:T(8,128)(2,1)S(1)} %fusion), channel_id=1, source_target_pairs={{0,8},{4,12},{8,16},{12,20},{16,24},{20,28},{1,9},{5,13},{9,17},{1... | collective-permute-start | bytes 6291464 | tf_op jit(solution)/shard_map/ppermute | solution.py:12
  24.6 92.8 %collective-permute-start.2 = (bf16[2,512,1024]{2,1,0:T(8,128)(2,1)S(1)}, bf16[2,512,1024]{2,1,0:T(8,128)(2,1)S(1)}, u32[]{:S(2)}, u32[]{:S(2)}) collective-permute-start(bf16[2,512,1024]{2,1,0:T(8,128)(2,1)S(1)} %fusion), channel_id=1, source_target_pairs={{0,12},{4,16},{8,20},{12,24},{16,28},{1,13},{5,17},{9,21},{13,25},... | collective-permute-start | bytes 6291464 | tf_op jit(solution)/shard_map/ppermute | solution.py:12
  26.8 178.1 %collective-permute-start = (bf16[2,512,1024]{2,1,0:T(8,128)(2,1)S(1)}, bf16[2,512,1024]{2,1,0:T(8,128)(2,1)S(1)}, u32[]{:S(2)}, u32[]{:S(2)}) collective-permute-start(bf16[2,512,1024]{2,1,0:T(8,128)(2,1)S(1)} %fusion), channel_id=1, source_target_pairs={{0,4},{4,8},{8,12},{12,16},{16,20},{20,24},{24,28},{1,5},{5,9},{9,... | collective-permute-start | bytes 6291464 | tf_op jit(solution)/shard_map/ppermute | solution.py:12
Sparse Core Ops, SparseCore 0:
  216.4 70.8 reduce-scatter.1
where the time goes:
time: 303 us; the launch traced here: 302 us
  waiting for transfers between devices  235 us (78%)
  other arithmetic  21.4 us (7%)
  between operations  13.5 us (4%)
  matrix products  10 us (3%)
  starting transfers between devices  8.36 us (3%)
  blocking collectives  6.93 us (2%)
  local copies, waits for them, and re-layouts  5.93 us (2%)
    ppermute x3, waiting for transfers between devices, shifted(): return lax.ppermute(block, axis, route)  164 us
    reduce_scatter x1, waiting for transfers between devices, on_device(): lax.psum_scatter(jnp.stack(pieces, axis=1).astype(jnp.bfloat16), 'win', s...  71 us
    dot_general x4, matrix products, cross_rows(): jnp.einsum('fwi,fwj->fij', left, partner, preferred_element_type=jnp.floa...  10 us
    ppermute x3, starting transfers between devices, shifted(): return lax.ppermute(block, axis, route)  8.36 us
    another operation x4, other arithmetic, on_device(): jnp.stack(pieces, axis=1).astype(jnp.bfloat16)  7.86 us
    psum x1, blocking collectives, on_device(): energy = lax.psum(power, 'win')  6.93 us
  transfers between devices with their start and end apart: 4, of which 4 were waited for; matrix products, arithmetic and copies ran while one was open for 4% of the time, Pallas kernels for 0%

commit v1 on v0

v1 whole, which is shorter than its diff:
```python
import functools

import jax
import jax.numpy as jnp
from jax import lax
from jax.experimental import pallas as pl
from jax.experimental.pallas import tpu as pltpu
from jax.sharding import PartitionSpec as P

MESH = pl.DeviceIdType.MESH
LIFT = 2.0**40
EPS = 1e-06


def kernel(n_chan, n_win, windows, x_ref, near_ref, out_ref, blk, left, own, cs, cr, ys, yr, xs, xr,
           es, er, scale, column, bx_s, bx_r, bz_s, bz_r, c_s, c_r, y_s, y_r, r_s, r_r, e_s, e_r):
    depth, width = x_ref.shape[2], x_ref.shape[3]
    rows = width // n_win
    n_y = n_win // 2
    chan, win = lax.axis_index("chan"), lax.axis_index("win")
    p, pair = lax.rem(chan, 2), chan // 2
    core, y = lax.rem(win, 2), win // 2
    has_up = pair < n_chan // 2 - 1
    has_down = pair >= 1
    has_down2 = pair >= 2
    mate = (chan + 1 - 2 * p, win)
    up, down = (chan + 2, win), (chan - 2, win)
    twin = (chan, win + 1 - 2 * core)

    def win_peer(d):
        return (chan, lax.rem(win + d, n_win))

    def y_peer(d):
        return lax.rem(y + d, n_y)

    def remote(src, dst, ss, rs, to):
        return pltpu.make_async_remote_copy(
            src_ref=src, dst_ref=dst, send_sem=ss, recv_sem=rs, device_id=to, device_id_type=MESH)

    def exchange():
        return remote(x_ref.at[:, 1 - p], blk.at[p], bx_s, bx_r, mate)

    def exchanged():
        return remote(x_ref.at[:, p], blk.at[1 - p], bx_s, bx_r, mate)

    def climb(src, dst, n):
        return remote(blk.at[src], blk.at[dst], bz_s.at[n], bz_r.at[n], up)

    def core_copy(k):
        return remote(cs.at[k], cr.at[k], c_s.at[k], c_r.at[k], twin)

    def y_copy(k, d):
        return remote(ys.at[k, d - 1], yr.at[k, d - 1], y_s.at[k, d - 1], y_r.at[k, d - 1],
                      (chan, y_peer(d) * 2 + core))

    def result_copy(r):
        return remote(xs.at[r], xr.at[r], r_s.at[r], r_r.at[r], mate)

    def energy_copy(s, d):
        return remote(es.at[s], er.at[s, d - 1], e_s.at[s, d - 1], e_r.at[s, d - 1], win_peer(d))

    barrier = pltpu.get_barrier_semaphore()

    def greet(to):
        pl.semaphore_signal(barrier, inc=1, device_id=to, device_id_type=MESH)

    greet(mate)
    for d in range(1, n_win):
        greet(win_peer(d))
    pl.when(has_up)(lambda: greet(up))
    pl.when(has_down)(lambda: greet(down))
    pl.semaphore_wait(barrier, n_win + has_up.astype(jnp.int32) + has_down.astype(jnp.int32))

    exchange().start()
    blk[p] = x_ref[:, p]
    pl.when(has_up)(lambda: climb(p, 2 + p, 0).start())

    def energy(s):
        def step(i, total):
            part = blk[s, :, pl.ds(pl.multiple_of(i * 64, 64), 64)].astype(jnp.float32)
            return total + jnp.sum((part * part).reshape(2 * 8, 8, width), axis=0)

        total = lax.fori_loop(0, depth // 64, step, jnp.zeros((8, width), jnp.float32))
        es[s] = jnp.broadcast_to(jnp.sum(total, axis=0, keepdims=True), (8, width))
        for d in range(1, n_win):
            energy_copy(s, d).start()

    def finish_energy(s):
        total = es[s]
        for d in range(1, n_win):
            energy_copy(s, d).wait_recv()
            total = total + er[s, d - 1]
        scale[s] = lax.rsqrt(total / windows + EPS)

    def finish_column(kb):
        row = lax.broadcasted_iota(jnp.int32, (rows, width), 0) + win * rows
        lane = lax.broadcasted_iota(jnp.int32, (rows, width), 1)
        wide = jnp.broadcast_to(scale[kb, 0:1], (rows, width))
        picked = jnp.sum(jnp.where(row == lane, wide, 0.0), axis=1, keepdims=True)
        column[kb] = jnp.broadcast_to(picked * (1.0 / (LIFT * windows)), (rows, 128))

    def build_left(kb):
        lift = jnp.asarray(LIFT, jnp.bfloat16)
        real = (blk[kb, 0] * lift).T
        imag = (blk[kb, 1] * lift).T
        for q in range(n_win):
            base = ((q % 2) * n_y + q // 2) * 2 * rows
            cut = slice(q * rows, (q + 1) * rows)
            left[kb, base:base + rows, :depth] = real[cut]
            left[kb, base:base + rows, depth:] = imag[cut]
            left[kb, base + rows:base + 2 * rows, :depth] = -imag[cut]
            left[kb, base + rows:base + 2 * rows, depth:] = real[cut]

    def product(kb, r, s):
        k = kb * 4 + r
        right = blk[s].reshape(2 * depth, width)
        far = pl.multiple_of((1 - core) * width, width)
        near_by = pl.multiple_of(core * width, width)
        cs[k] = jnp.dot(left[kb, pl.ds(far, width)], right, preferred_element_type=jnp.float32).astype(jnp.bfloat16)
        core_copy(k).start()
        own[k] = jnp.dot(left[kb, pl.ds(near_by, width)], right, preferred_element_type=jnp.float32)

    def fold(kb, r, s):
        k = kb * 4 + r
        core_copy(k).wait_recv()
        for d in range(1, n_y):
            cut = pl.ds(pl.multiple_of(y_peer(d) * 2 * rows, 2 * rows), 2 * rows)
            ys[k, d - 1] = (own[k, cut] + cr[k, cut].astype(jnp.float32)).astype(jnp.bfloat16)
            y_copy(k, d).start()

    def weight(r):
        value = near_ref[0, jnp.maximum(r - 1, 0)]
        return jnp.where(r == 0, 1.0, value.astype(jnp.float32))

    def final(kb, r, s):
        k = kb * 4 + r
        cut = pl.ds(pl.multiple_of(y * 2 * rows, 2 * rows), 2 * rows)
        total = own[k, cut] + cr[k, cut].astype(jnp.float32)
        for d in range(1, n_y):
            y_copy(k, d).wait_recv()
            total = total + yr[k, d - 1].astype(jnp.float32)
        col = column[kb][:, 0:1]
        total = total.reshape(2, rows, width) * (col * scale[s, 0:1])[None]

        @pl.when(kb == p)
        def _():
            out_ref[r, :, p] = total * weight(r)

        @pl.when(kb != p)
        def _():
            xs[r] = total.astype(jnp.bfloat16)
            result_copy(r).start()

    groups = (
        (1, lambda n: (p, 0 * n, p)),
        (2, lambda n: (1 - p + n * p, n, (1 - p) * (1 - n))),
        (2, lambda n: (n, 2 - p + n, 2 + p)),
        (2, lambda n: (n, 1 + p + n, 3 - p)),
        (1, lambda n: (0 * n, 0 * n + 3, 0 * n + 4)),
    )

    def each(work, g):
        count, params = groups[g]

        def step(n, carry):
            work(*params(n))
            return carry

        lax.fori_loop(0, count, step, 0)

    energy(p)
    build_left(p)
    each(product, 0)
    exchanged().wait_recv()
    pl.when(has_up)(lambda: climb(1 - p, 3 - p, 1).start())
    build_left(1 - p)
    each(product, 1)
    each(fold, 0)
    each(fold, 1)
    energy(1 - p)

    @pl.when(has_down)
    def _():
        climb(p, 2 + p, 0).wait_recv()
        each(product, 2)
        each(fold, 2)
        energy(2 + p)

    for s in range(2):
        finish_energy(s)
        finish_column(s)
    each(final, 0)
    each(final, 1)

    @pl.when(has_down)
    def _():
        climb(1 - p, 3 - p, 1).wait_recv()
        pl.when(has_up)(lambda: climb(3, 4, 2).start())
        each(product, 3)
        each(fold, 3)
        energy(3 - p)
        finish_energy(2)
        finish_energy(3)
        each(final, 2)

    @pl.when(has_down2)
    def _():
        climb(3, 4, 2).wait_recv()
        each(product, 4)
        each(fold, 4)
        energy(4)

    pl.when(has_down)(lambda: each(final, 3))

    @pl.when(has_down2)
    def _():
        finish_energy(4)
        each(final, 4)

    def receive(r, carry):
        @pl.when(chan >= r)
        def _():
            result_copy(r).wait_recv()
            out_ref[r, :, 1 - p] = xr[r].astype(jnp.float32) * weight(r)

        @pl.when(chan < r)
        def _():
            out_ref[r] = jnp.zeros(out_ref.shape[1:], jnp.float32)

        return carry

    lax.fori_loop(0, 4, receive, 0)

    exchange().wait_send()

    @pl.when(has_up)
    def _():
        climb(p, 2 + p, 0).wait_send()
        climb(1 - p, 3 - p, 1).wait_send()
        pl.when(has_down)(lambda: climb(3, 4, 2).wait_send())

    def sent(kb, r, s):
        core_copy(kb * 4 + r).wait_send()
        for d in range(1, n_y):
            y_copy(kb * 4 + r, d).wait_send()
        pl.when(kb != p)(lambda: result_copy(r).wait_send())

    def energy_sent(s):
        for d in range(1, n_win):
            energy_copy(s, d).wait_send()

    each(sent, 0)
    each(sent, 1)
    energy_sent(0)
    energy_sent(1)

    @pl.when(has_down)
    def _():
        each(sent, 2)
        each(sent, 3)
        energy_sent(2)
        energy_sent(3)

    @pl.when(has_down2)
    def _():
        each(sent, 4)
        energy_sent(4)


def on_device(n_chan, n_win, spectra, near):
    _, freqs, depth, width = spectra.shape
    rounds = near.shape[1] + 1
    rows, n_y = width // n_win, n_win // 2
    bf, f32 = jnp.bfloat16, jnp.float32
    dma = pltpu.SemaphoreType.DMA
    out = pl.pallas_call(
        functools.partial(kernel, n_chan, n_win, float(depth * n_win)),
        out_shape=jax.ShapeDtypeStruct((rounds, 2, freqs, rows, width), f32),
        in_specs=[pl.BlockSpec(memory_space=pltpu.VMEM), pl.BlockSpec(memory_space=pltpu.SMEM)],
        out_specs=pl.BlockSpec(memory_space=pltpu.VMEM),
        scratch_shapes=[
            pltpu.VMEM((5, 2, depth, width), bf),
            pltpu.VMEM((2, 2 * width, 2 * depth), bf),
            pltpu.VMEM((8, width, width), f32),
            pltpu.VMEM((8, width, width), bf),
            pltpu.VMEM((8, width, width), bf),
            pltpu.VMEM((8, n_y - 1, 2 * rows, width), bf),
            pltpu.VMEM((8, n_y - 1, 2 * rows, width), bf),
            pltpu.VMEM((rounds, 2, rows, width), bf),
            pltpu.VMEM((rounds, 2, rows, width), bf),
            pltpu.VMEM((5, 8, width), f32),
            pltpu.VMEM((5, n_win - 1, 8, width), f32),
            pltpu.VMEM((5, 8, width), f32),
            pltpu.VMEM((2, rows, 128), f32),
            dma, dma, dma((3,)), dma((3,)), dma((8,)), dma((8,)),
            dma((8, n_y - 1)), dma((8, n_y - 1)), dma((rounds,)), dma((rounds,)),
            dma((5, n_win - 1)), dma((5, n_win - 1)),
        ],
        compiler_params=pltpu.CompilerParams(
            collective_id=0, has_side_effects=True, vmem_limit_bytes=56 * 1024 * 1024),
        cost_estimate=pl.CostEstimate(
            flops=64 * depth * width * width, bytes_accessed=6 * 1024 * 1024, transcendentals=0),
    )(spectra, near)
    return jnp.transpose(out, (3, 0, 1, 2, 4))


def solution(mesh):
    sizes = dict(mesh.shape)
    return jax.shard_map(
        functools.partial(on_device, sizes["chan"], sizes["win"]),
        mesh=mesh,
        in_specs=(P(None, None, "win", "chan"), P("chan", None)),
        out_specs=P(("chan", "win"), None, None, None, None),
        check_vma=False,
    )
```

time: 303 us -> 104 us (0.34)
  waiting for transfers between devices: 235 us -> 0 us
  Pallas kernels: 0 us -> 96.6 us
  other arithmetic: 21.4 us -> 0 us
  between operations: 13.5 us -> 0.01 us
  matrix products: 10 us -> 0 us
  starting transfers between devices: 8.36 us -> 0 us
  blocking collectives: 6.93 us -> 0 us
    ppermute x3 -> x0, waiting for transfers between devices: 164 us -> none  [shifted(): return lax.ppermute(block, axis, route)]
    pallas_call x0 -> x1, Pallas kernels: none -> 96.6 us  [on_device(): pl.pallas_call(functools.partial(kernel, n_chan, n_win, float(depth * n_w...]
    reduce_scatter x1 -> x0, waiting for transfers between devices: 71 us -> none  [on_device(): lax.psum_scatter(jnp.stack(pieces, axis=1).astype(jnp.bfloat16), 'win', s...]
    another operation x8 -> x0, other arithmetic: 11.7 us -> none  [the longest x4 7.86 us: on_device(): jnp.stack(pieces, axis=1).astype(jnp.bfloat16)]
    dot_general x4 -> x0, matrix products: 10 us -> none  [cross_rows(): jnp.einsum('fwi,fwj->fij', left, partner, preferred_element_type=jnp.floa...]
    ppermute x3 -> x0, starting transfers between devices: 8.36 us -> none  [shifted(): return lax.ppermute(block, axis, route)]
    transpose x0 -> x1, local copies, waits for them, and re-layouts: none -> 7.44 us  [on_device(): return jnp.transpose(out, (3, 0, 1, 2, 4))]
    convert_element_type x3 -> x0, other arithmetic: 7.13 us -> none  [the longest x1 4.32 us: on_device(): real_part = spectra[0].astype(jnp.float32)]
  transfers between devices with their start and end apart: 4 -> 0, of which waited for: 4 -> 0; matrix products, arithmetic and copies ran while one was open for 4% -> 0% of each run, Pallas kernels for 0% -> 0%
where the time goes in v1:
time: 104 us
  Pallas kernels  96.6 us (93%)
  local copies, waits for them, and re-layouts  7.44 us (7%)
    pallas_call x1, Pallas kernels, on_device(): pl.pallas_call(functools.partial(kernel, n_chan, n_win, float(depth * n_w...  96.6 us
    transpose x1, local copies, waits for them, and re-layouts, on_device(): return jnp.transpose(out, (3, 0, 1, 2, 4))  7.44 us

profile of v1, /device:TPU:16, one launch (start us, length us, event | category | flops | bytes accessed | tf_op | source)
XLA Modules:
  0.0 104.1 jit_solution(11205070037871224805)
XLA Ops:
  0.0 96.6 %shard_map.28 = f32[4,2,2,128,512]{4,3,2,1,0:T(8,128)} custom-call(bf16[2,2,512,512]{3,2,1,0:T(8,128)(2,1)} %x_ref.1, s32[1,3]{1,0:T(1,128)} %near_ref.1), custom_call_target="tpu_custom_call" | custom-call | flops 8589934592 | bytes 6291456 | tf_op jit(solution)/shard_map/pallas_call | solution.py:276
  96.6 7.4 %copy.3 = f32[128,4,2,2,512]{4,3,2,1,0:T(2,128)} copy(f32[128,4,2,2,512]{4,0,3,2,1:T(8,128)} %bitcast.1) | data formatting | bytes 8388608 | tf_op jit(solution)/shard_map/transpose | solution.py:304

commit v2 on v1

v2 whole, which is shorter than its diff:
```python
import functools

import jax
import jax.numpy as jnp
from jax import lax
from jax.experimental import pallas as pl
from jax.experimental.pallas import tpu as pltpu
from jax.sharding import PartitionSpec as P

MESH = pl.DeviceIdType.MESH
LIFT = 2.0**40
EPS = 1e-06


def kernel(n_chan, n_win, windows, x_ref, near_ref, out_ref, blk, left, own, cs, cr, ys, yr, xs, xr,
           es, er, scale, column, bx_s, bx_r, bu_s, bu_r, bd_s, bd_r, c_s, c_r, y_s, y_r, r_s, r_r,
           e_s, e_r):
    depth, width = x_ref.shape[2], x_ref.shape[3]
    rows = width // n_win
    n_y = n_win // 2
    chan, win = lax.axis_index("chan"), lax.axis_index("win")
    p, pair = lax.rem(chan, 2), chan // 2
    core, y = lax.rem(win, 2), win // 2
    has_up = pair < n_chan // 2 - 1
    has_down = pair >= 1
    has_both = jnp.logical_and(has_up, has_down)
    even, odd = p == 0, p == 1
    mate = (chan + 1 - 2 * p, win)
    up, down = (chan + 2, win), (chan - 2, win)
    up_mate, down_mate = (chan + 3 - 2 * p, win), (chan - 1 - 2 * p, win)
    twin = (chan, win + 1 - 2 * core)

    def win_peer(d):
        return (chan, lax.rem(win + d, n_win))

    def y_peer(d):
        return lax.rem(y + d, n_y)

    def remote(src, dst, ss, rs, to):
        return pltpu.make_async_remote_copy(
            src_ref=src, dst_ref=dst, send_sem=ss, recv_sem=rs, device_id=to, device_id_type=MESH)

    def exchange(c):
        return remote(x_ref.at[c, 1 - p], blk.at[p, c], bx_s.at[c], bx_r.at[c], mate)

    def exchanged(c):
        return remote(x_ref.at[c, p], blk.at[1 - p, c], bx_s.at[c], bx_r.at[c], mate)

    def climb(c):
        return remote(blk.at[1, c], blk.at[2, c], bu_s.at[c], bu_r.at[c], up)

    def descend(slot, n):
        return remote(blk.at[slot], blk.at[3 + slot], bd_s.at[n], bd_r.at[n], down)

    def core_copy(k):
        return remote(cs.at[k], cr.at[k], c_s.at[k], c_r.at[k], twin)

    def y_copy(k, d):
        return remote(ys.at[k, d - 1], yr.at[k, d - 1], y_s.at[k, d - 1], y_r.at[k, d - 1],
                      (chan, y_peer(d) * 2 + core))

    def result_copy(m, r, w, to):
        return remote(xs.at[m], xr.at[r, w], r_s.at[m], r_r.at[r, w], to)

    def energy_copy(s, d):
        return remote(es.at[s], er.at[s, d - 1], e_s.at[s, d - 1], e_r.at[s, d - 1], win_peer(d))

    barrier = pltpu.get_barrier_semaphore()

    def greet(*others):
        for to in others:
            pl.semaphore_signal(barrier, inc=1, device_id=to, device_id_type=MESH)

    greet(mate)
    for d in range(1, n_win):
        greet(win_peer(d))
    pl.when(has_up)(lambda: greet(up, up_mate))
    pl.when(has_down)(lambda: greet(down, down_mate))
    pl.semaphore_wait(barrier, n_win + 2 * (has_up.astype(jnp.int32) + has_down.astype(jnp.int32)))

    for c in range(2):
        exchange(c).start()
    blk[p] = x_ref[:, p]

    @pl.when(has_down)
    def _():
        descend(p, 0).start()

    @pl.when(jnp.logical_and(has_up, odd))
    def _():
        for c in range(2):
            climb(c).start()

    def energy(s):
        def step(i, total):
            part = blk[s, :, pl.ds(pl.multiple_of(i * 64, 64), 64)].astype(jnp.float32)
            return total + jnp.sum((part * part).reshape(2 * 8, 8, width), axis=0)

        total = lax.fori_loop(0, depth // 64, step, jnp.zeros((8, width), jnp.float32))
        es[s] = jnp.broadcast_to(jnp.sum(total, axis=0, keepdims=True), (8, width))
        for d in range(1, n_win):
            energy_copy(s, d).start()

    def finish_energy(s):
        total = es[s]
        for d in range(1, n_win):
            energy_copy(s, d).wait_recv()
            total = total + er[s, d - 1]
        scale[s] = lax.rsqrt(total / windows + EPS)

    def finish_column(kb, s):
        row = lax.broadcasted_iota(jnp.int32, (rows, width), 0) + win * rows
        lane = lax.broadcasted_iota(jnp.int32, (rows, width), 1)
        wide = jnp.broadcast_to(scale[s, 0:1], (rows, width))
        picked = jnp.sum(jnp.where(row == lane, wide, 0.0), axis=1, keepdims=True)
        column[kb] = jnp.broadcast_to(picked * (1.0 / (LIFT * windows)), (rows, 128))

    def build_left(kb, s):
        lift = jnp.asarray(LIFT, jnp.bfloat16)
        real = (blk[s, 0] * lift).T
        imag = (blk[s, 1] * lift).T
        for q in range(n_win):
            base = ((q % 2) * n_y + q // 2) * 2 * rows
            cut = slice(q * rows, (q + 1) * rows)
            left[kb, base:base + rows, :depth] = real[cut]
            left[kb, base:base + rows, depth:] = imag[cut]
            left[kb, base + rows:base + 2 * rows, :depth] = -imag[cut]
            left[kb, base + rows:base + 2 * rows, depth:] = real[cut]

    def product(m, kb, s, q, r):
        right = blk[s].reshape(2 * depth, width)
        far = pl.multiple_of((1 - core) * width, width)
        near_by = pl.multiple_of(core * width, width)
        cs[m] = jnp.dot(left[kb, pl.ds(far, width)], right, preferred_element_type=jnp.float32).astype(jnp.bfloat16)
        core_copy(m).start()
        own[m] = jnp.dot(left[kb, pl.ds(near_by, width)], right, preferred_element_type=jnp.float32)

    def fold(m, kb, s, q, r):
        core_copy(m).wait_recv()
        for d in range(1, n_y):
            cut = pl.ds(pl.multiple_of(y_peer(d) * 2 * rows, 2 * rows), 2 * rows)
            ys[m, d - 1] = (own[m, cut] + cr[m, cut].astype(jnp.float32)).astype(jnp.bfloat16)
            y_copy(m, d).start()

    def weight(r):
        value = near_ref[0, jnp.maximum(r - 1, 0)]
        return jnp.where(r == 0, 1.0, value.astype(jnp.float32))

    def store(r, f, value):
        out_ref[r, :, f] = value * weight(r)

    def total_of(m, kb, s):
        cut = pl.ds(pl.multiple_of(y * 2 * rows, 2 * rows), 2 * rows)
        total = own[m, cut] + cr[m, cut].astype(jnp.float32)
        for d in range(1, n_y):
            y_copy(m, d).wait_recv()
            total = total + yr[m, d - 1].astype(jnp.float32)
        return total.reshape(2, rows, width) * (column[kb][:, 0:1] * scale[s, 0:1])[None]

    def final_here(m, kb, s, q, r):
        total = total_of(m, kb, s)

        @pl.when(q == p)
        def _():
            store(r, p, total)

        @pl.when(q != p)
        def _():
            xs[m] = total.astype(jnp.bfloat16)
            result_copy(m, r, 0, mate).start()

    def target_up(m, r, q):
        same = (q == p).astype(jnp.int32)
        return result_copy(m, r, same, (chan - p + 2 + q, win))

    def final_up(m, kb, s, q, r):
        xs[m] = total_of(m, kb, s).astype(jnp.bfloat16)
        target_up(m, r, q).start()

    groups = dict(
        mine=(1, lambda n: (p, p, p, p, 0 * n)),
        pair=(2, lambda n: (1 - p + n * (1 + p), 1 - p + n * p, (1 - p) * (1 - n), 1 - p + n * p, n)),
        above=(1, lambda n: (5 + p + 0 * n, 2 + p, 0 * n, p, 2 + p)),
        below=(2, lambda n: (3 + n, n, 0 * n + 2, n, 1 + n)),
        other=(1, lambda n: (6 - p + 0 * n, 3 - p, 0 * n, 1 - p, 3 - p)),
        span=(1, lambda n: (0 * n + 7, 0 * n + 2, 0 * n + 2, 0 * n, 0 * n + 3)),
    )

    def each(work, g):
        count, params = groups[g]

        def step(n, carry):
            work(*params(n))
            return carry

        lax.fori_loop(0, count, step, 0)

    def make(g):
        each(product, g)
        each(fold, g)

    build_left(p, p)
    each(product, "mine")
    energy(p)
    each(fold, "mine")
    for c in range(2):
        exchanged(c).wait_recv()
        pl.when(jnp.logical_and(has_up, even))(lambda: climb(c).start())
    pl.when(has_down)(lambda: descend(1 - p, 1).start())
    build_left(1 - p, 1 - p)
    make("pair")
    energy(1 - p)

    @pl.when(has_up)
    def _():
        descend(p, 0).wait_recv()
        build_left(2 + p, 3 + p)
        make("above")
        energy(3 + p)

    for s in range(2):
        finish_energy(s)
        finish_column(s, s)
    each(final_here, "mine")

    @pl.when(has_down)
    def _():
        for c in range(2):
            climb(c).wait_recv()
        make("below")
        energy(2)

    pl.when(jnp.logical_and(has_both, even))(lambda: make("span"))
    each(final_here, "pair")

    @pl.when(has_up)
    def _():
        finish_energy(3 + p)
        finish_column(2 + p, 3 + p)
        each(final_up, "above")
        descend(1 - p, 1).wait_recv()
        build_left(3 - p, 4 - p)
        make("other")
        energy(4 - p)

    pl.when(jnp.logical_and(has_both, odd))(lambda: make("span"))

    @pl.when(has_down)
    def _():
        finish_energy(2)
        each(final_here, "below")

    @pl.when(has_up)
    def _():
        finish_energy(4 - p)
        finish_column(3 - p, 4 - p)
        each(final_up, "other")

    pl.when(has_both)(lambda: each(final_up, "span"))

    def receive(r, carry):
        @pl.when(chan >= r)
        def _():
            result_copy(0, r, 0, mate).wait_recv()
            store(r, 1 - p, xr[r, 0].astype(jnp.float32).reshape(2, rows, width))

        @pl.when(jnp.logical_and(chan >= r, r >= 2 + p))
        def _():
            result_copy(0, r, 1, mate).wait_recv()
            store(r, p, xr[r, 1].astype(jnp.float32).reshape(2, rows, width))

        @pl.when(chan < r)
        def _():
            out_ref[r] = jnp.zeros(out_ref.shape[1:], jnp.float32)

        return carry

    lax.fori_loop(0, 4, receive, 0)

    for c in range(2):
        exchange(c).wait_send()

    @pl.when(has_up)
    def _():
        for c in range(2):
            climb(c).wait_send()

    @pl.when(has_down)
    def _():
        descend(p, 0).wait_send()
        descend(1 - p, 1).wait_send()

    def sent(m, kb, s, q, r):
        core_copy(m).wait_send()
        for d in range(1, n_y):
            y_copy(m, d).wait_send()

    def sent_here(m, kb, s, q, r):
        sent(m, kb, s, q, r)
        pl.when(q != p)(lambda: result_copy(m, r, 0, mate).wait_send())

    def sent_up(m, kb, s, q, r):
        sent(m, kb, s, q, r)
        target_up(m, r, q).wait_send()

    def energy_sent(s):
        for d in range(1, n_win):
            energy_copy(s, d).wait_send()

    each(sent_here, "mine")
    each(sent_here, "pair")
    energy_sent(0)
    energy_sent(1)

    @pl.when(has_down)
    def _():
        each(sent_here, "below")
        energy_sent(2)

    @pl.when(has_up)
    def _():
        each(sent_up, "above")
        each(sent_up, "other")
        energy_sent(3)
        energy_sent(4)

    pl.when(has_both)(lambda: each(sent_up, "span"))


def on_device(n_chan, n_win, spectra, near):
    _, freqs, depth, width = spectra.shape
    rounds = near.shape[1] + 1
    rows, n_y = width // n_win, n_win // 2
    bf, f32 = jnp.bfloat16, jnp.float32
    dma = pltpu.SemaphoreType.DMA
    out = pl.pallas_call(
        functools.partial(kernel, n_chan, n_win, float(depth * n_win)),
        out_shape=jax.ShapeDtypeStruct((rounds, 2, freqs, rows, width), f32),
        in_specs=[pl.BlockSpec(memory_space=pltpu.VMEM), pl.BlockSpec(memory_space=pltpu.SMEM)],
        out_specs=pl.BlockSpec(memory_space=pltpu.VMEM),
        scratch_shapes=[
            pltpu.VMEM((5, 2, depth, width), bf),
            pltpu.VMEM((4, 2 * width, 2 * depth), bf),
            pltpu.VMEM((8, width, width), f32),
            pltpu.VMEM((8, width, width), bf),
            pltpu.VMEM((8, width, width), bf),
            pltpu.VMEM((8, n_y - 1, 2 * rows, width), bf),
            pltpu.VMEM((8, n_y - 1, 2 * rows, width), bf),
            pltpu.VMEM((8, 2, rows, width), bf),
            pltpu.VMEM((rounds, 2, 2, rows, width), bf),
            pltpu.VMEM((5, 8, width), f32),
            pltpu.VMEM((5, n_win - 1, 8, width), f32),
            pltpu.VMEM((5, 8, width), f32),
            pltpu.VMEM((4, rows, 128), f32),
            dma((2,)), dma((2,)), dma((2,)), dma((2,)), dma((2,)), dma((2,)), dma((8,)), dma((8,)),
            dma((8, n_y - 1)), dma((8, n_y - 1)), dma((8,)), dma((rounds, 2)),
            dma((5, n_win - 1)), dma((5, n_win - 1)),
        ],
        compiler_params=pltpu.CompilerParams(
            collective_id=0, has_side_effects=True, vmem_limit_bytes=56 * 1024 * 1024),
        cost_estimate=pl.CostEstimate(
            flops=64 * depth * width * width, bytes_accessed=6 * 1024 * 1024, transcendentals=0),
    )(spectra, near)
    return jnp.transpose(out, (3, 0, 1, 2, 4))


def solution(mesh):
    sizes = dict(mesh.shape)
    return jax.shard_map(
        functools.partial(on_device, sizes["chan"], sizes["win"]),
        mesh=mesh,
        in_specs=(P(None, None, "win", "chan"), P("chan", None)),
        out_specs=P(("chan", "win"), None, None, None, None),
        check_vma=False,
    )
```

time: 104 us -> 98.7 us (0.949)
  Pallas kernels: 96.6 us -> 91.1 us
    pallas_call x1, Pallas kernels: 96.6 us -> 91.1 us  [on_device(): pl.pallas_call(functools.partial(kernel, n_chan, n_win, float(depth * n_w...]
where the time goes in v2:
time: 98.7 us; the launch traced here: 98.6 us
  Pallas kernels  91.1 us (92%)
  local copies, waits for them, and re-layouts  7.44 us (8%)
    pallas_call x1, Pallas kernels, on_device(): pl.pallas_call(functools.partial(kernel, n_chan, n_win, float(depth * n_w...  91.1 us
    transpose x1, local copies, waits for them, and re-layouts, on_device(): return jnp.transpose(out, (3, 0, 1, 2, 4))  7.44 us

profile of v2, /device:TPU:16, one launch (start us, length us, event | category | flops | bytes accessed | tf_op | source)
XLA Modules:
  0.0 98.6 jit_solution(17766026200801417950)
XLA Ops:
  0.0 91.1 %shard_map.28 = f32[4,2,2,128,512]{4,3,2,1,0:T(8,128)} custom-call(bf16[2,2,512,512]{3,2,1,0:T(8,128)(2,1)} %x_ref.1, s32[1,3]{1,0:T(1,128)} %near_ref.1), custom_call_target="tpu_custom_call" | custom-call | flops 8589934592 | bytes 6291456 | tf_op jit(solution)/shard_map/pallas_call | solution.py:336
  91.1 7.4 %copy.3 = f32[128,4,2,2,512]{4,3,2,1,0:T(2,128)} copy(f32[128,4,2,2,512]{4,0,3,2,1:T(8,128)} %bitcast.1) | data formatting | bytes 8388608 | tf_op jit(solution)/shard_map/transpose | solution.py:364

commit v3 on v2

--- a/solution.py
+++ b/solution.py
@@ -18,6 +18,7 @@
     depth, width = x_ref.shape[2], x_ref.shape[3]
     rows = width // n_win
     n_y = n_win // 2
+    step_rows = out_ref.shape[0] // rows
     chan, win = lax.axis_index("chan"), lax.axis_index("win")
     p, pair = lax.rem(chan, 2), chan // 2
     core, y = lax.rem(win, 2), win // 2
@@ -147,7 +148,11 @@
         return jnp.where(r == 0, 1.0, value.astype(jnp.float32))
 
     def store(r, f, value):
-        out_ref[r, :, f] = value * weight(r)
+        value = value * weight(r)
+        for c in range(2):
+            for tile in range(width // 128):
+                at = pl.ds(((r * 2 + c) * (width // 128) + tile) * 2 + f, rows, stride=step_rows)
+                out_ref[at, :] = value[c, :, tile * 128:(tile + 1) * 128]
 
     def total_of(m, kb, s):
         cut = pl.ds(pl.multiple_of(y * 2 * rows, 2 * rows), 2 * rows)
@@ -169,6 +174,9 @@
             xs[m] = total.astype(jnp.bfloat16)
             result_copy(m, r, 0, mate).start()
 
+    def final_twist(m, kb, s, q, r):
+        store(r, 1 - p, total_of(m, kb, s))
+
     def target_up(m, r, q):
         same = (q == p).astype(jnp.int32)
         return result_copy(m, r, same, (chan - p + 2 + q, win))
@@ -178,8 +186,9 @@
         target_up(m, r, q).start()
 
     groups = dict(
-        mine=(1, lambda n: (p, p, p, p, 0 * n)),
-        pair=(2, lambda n: (1 - p + n * (1 + p), 1 - p + n * p, (1 - p) * (1 - n), 1 - p + n * p, n)),
+        mine=(1, lambda n: (0 * n, p, p, p, 0 * n)),
+        twist=(1, lambda n: (0 * n + 1, 0 * n + 4, 0 * n + 5, p, 0 * n)),
+        pair=(1, lambda n: (0 * n + 2, 0 * n + 1, 0 * n, 0 * n + 1, 0 * n + 1)),
         above=(1, lambda n: (5 + p + 0 * n, 2 + p, 0 * n, p, 2 + p)),
         below=(2, lambda n: (3 + n, n, 0 * n + 2, n, 1 + n)),
         other=(1, lambda n: (6 - p + 0 * n, 3 - p, 0 * n, 1 - p, 3 - p)),
@@ -201,8 +210,13 @@
 
     build_left(p, p)
     each(product, "mine")
+    blk[5] = x_ref[:, 1 - p]
+    build_left(4, 5)
+    each(product, "twist")
+    each(fold, "mine")
+    each(fold, "twist")
     energy(p)
-    each(fold, "mine")
+    energy(5)
     for c in range(2):
         exchanged(c).wait_recv()
         pl.when(jnp.logical_and(has_up, even))(lambda: climb(c).start())
@@ -221,7 +235,10 @@
     for s in range(2):
         finish_energy(s)
         finish_column(s, s)
+    finish_energy(5)
+    finish_column(4, 5)
     each(final_here, "mine")
+    each(final_twist, "twist")
 
     @pl.when(has_down)
     def _():
@@ -259,7 +276,7 @@
     pl.when(has_both)(lambda: each(final_up, "span"))
 
     def receive(r, carry):
-        @pl.when(chan >= r)
+        @pl.when(jnp.logical_and(chan >= r, r >= 1))
         def _():
             result_copy(0, r, 0, mate).wait_recv()
             store(r, 1 - p, xr[r, 0].astype(jnp.float32).reshape(2, rows, width))
@@ -271,7 +288,8 @@
 
         @pl.when(chan < r)
         def _():
-            out_ref[r] = jnp.zeros(out_ref.shape[1:], jnp.float32)
+            for f in range(2):
+                store(r, f, jnp.zeros((2, rows, width), jnp.float32))
 
         return carry
 
@@ -307,10 +325,12 @@
         for d in range(1, n_win):
             energy_copy(s, d).wait_send()
 
-    each(sent_here, "mine")
+    each(sent, "mine")
+    each(sent, "twist")
     each(sent_here, "pair")
     energy_sent(0)
     energy_sent(1)
+    energy_sent(5)
 
     @pl.when(has_down)
     def _():
@@ -335,12 +355,12 @@
     dma = pltpu.SemaphoreType.DMA
     out = pl.pallas_call(
         functools.partial(kernel, n_chan, n_win, float(depth * n_win)),
-        out_shape=jax.ShapeDtypeStruct((rounds, 2, freqs, rows, width), f32),
+        out_shape=jax.ShapeDtypeStruct((rows * rounds * 2 * freqs * (width // 128), 128), f32),
         in_specs=[pl.BlockSpec(memory_space=pltpu.VMEM), pl.BlockSpec(memory_space=pltpu.SMEM)],
         out_specs=pl.BlockSpec(memory_space=pltpu.VMEM),
         scratch_shapes=[
-            pltpu.VMEM((5, 2, depth, width), bf),
-            pltpu.VMEM((4, 2 * width, 2 * depth), bf),
+            pltpu.VMEM((6, 2, depth, width), bf),
+            pltpu.VMEM((5, 2 * width, 2 * depth), bf),
             pltpu.VMEM((8, width, width), f32),
             pltpu.VMEM((8, width, width), bf),
             pltpu.VMEM((8, width, width), bf),
@@ -348,20 +368,21 @@
             pltpu.VMEM((8, n_y - 1, 2 * rows, width), bf),
             pltpu.VMEM((8, 2, rows, width), bf),
             pltpu.VMEM((rounds, 2, 2, rows, width), bf),
-            pltpu.VMEM((5, 8, width), f32),
-            pltpu.VMEM((5, n_win - 1, 8, width), f32),
-            pltpu.VMEM((5, 8, width), f32),
-            pltpu.VMEM((4, rows, 128), f32),
+            pltpu.VMEM((6, 8, width), f32),
+            pltpu.VMEM((6, n_win - 1, 8, width), f32),
+            pltpu.VMEM((6, 8, width), f32),
+            pltpu.VMEM((5, rows, 128), f32),
             dma((2,)), dma((2,)), dma((2,)), dma((2,)), dma((2,)), dma((2,)), dma((8,)), dma((8,)),
             dma((8, n_y - 1)), dma((8, n_y - 1)), dma((8,)), dma((rounds, 2)),
-            dma((5, n_win - 1)), dma((5, n_win - 1)),
+            dma((6, n_win - 1)), dma((6, n_win - 1)),
         ],
         compiler_params=pltpu.CompilerParams(
             collective_id=0, has_side_effects=True, vmem_limit_bytes=56 * 1024 * 1024),
         cost_estimate=pl.CostEstimate(
             flops=64 * depth * width * width, bytes_accessed=6 * 1024 * 1024, transcendentals=0),
     )(spectra, near)
-    return jnp.transpose(out, (3, 0, 1, 2, 4))
+    out = out.reshape(rows, rounds, 2, width // 128, freqs, 128)
+    return jnp.transpose(out, (0, 1, 2, 4, 3, 5)).reshape(rows, rounds, 2, freqs, width)
 
 
 def solution(mesh):

time: 98.7 us -> 92.8 us (0.940)
  Pallas kernels: 91.1 us -> 85.3 us
    transpose x1 -> x0, local copies, waits for them, and re-layouts: 7.44 us -> none  [on_device(): return jnp.transpose(out, (3, 0, 1, 2, 4))]
    unnamed x0 -> x1, local copies, waits for them, and re-layouts: none -> 7.34 us
    pallas_call x1, Pallas kernels: 91.1 us -> 85.3 us  [on_device(): pl.pallas_call(functools.partial(kernel, n_chan, n_win, float(depth * n_w...]
where the time goes in v3:
time: 92.8 us; the launch traced here: 92.6 us
  Pallas kernels  85.3 us (92%)
  local copies, waits for them, and re-layouts  7.34 us (8%)
    pallas_call x1, Pallas kernels, on_device(): pl.pallas_call(functools.partial(kernel, n_chan, n_win, float(depth * n_w...  85.3 us
    unnamed x1, local copies, waits for them, and re-layouts  7.34 us

profile of v3, /device:TPU:16, one launch (start us, length us, event | category | flops | bytes accessed | tf_op | source)
XLA Modules:
  0.0 92.6 jit_solution(1353417114842141676)
XLA Ops:
  0.0 85.3 %shard_map.28 = f32[8192,128]{1,0:T(8,128)} custom-call(bf16[2,2,512,512]{3,2,1,0:T(8,128)(2,1)} %x_ref.1, s32[1,3]{1,0:T(1,128)} %near_ref.1), custom_call_target="tpu_custom_call" | custom-call | flops 8589934592 | bytes 6291456 | tf_op jit(solution)/shard_map/pallas_call | solution.py:356
  85.3 7.3 %copy.5 = f32[128,4,2,2,512]{4,3,2,1,0:T(2,128)} copy(f32[128,4,2,2,512]{4,3,2,1,0:T(2,128)} %bitcast.5) | data formatting | bytes 8388608

commit v4 on v3

--- a/solution.py
+++ b/solution.py
@@ -12,13 +12,14 @@
 EPS = 1e-06
 
 
-def kernel(n_chan, n_win, windows, x_ref, near_ref, out_ref, blk, left, own, cs, cr, ys, yr, xs, xr,
+def kernel(n_chan, n_win, windows, x_ref, near_ref, result_ref, out_ref, blk, left, own, cs, cr, ys, yr, xs, xr,
            es, er, scale, column, bx_s, bx_r, bu_s, bu_r, bd_s, bd_r, c_s, c_r, y_s, y_r, r_s, r_r,
-           e_s, e_r):
+           e_s, e_r, in_s, out_s):
     depth, width = x_ref.shape[2], x_ref.shape[3]
     rows = width // n_win
     n_y = n_win // 2
-    step_rows = out_ref.shape[0] // rows
+    rounds, step_rows = result_ref.shape[1], result_ref.shape[1] * result_ref.shape[2]
+    flat = out_ref.reshape(rows * step_rows, 128)
     chan, win = lax.axis_index("chan"), lax.axis_index("win")
     p, pair = lax.rem(chan, 2), chan // 2
     core, y = lax.rem(win, 2), win // 2
@@ -50,8 +51,17 @@
     def climb(c):
         return remote(blk.at[1, c], blk.at[2, c], bu_s.at[c], bu_r.at[c], up)
 
-    def descend(slot, n):
-        return remote(blk.at[slot], blk.at[3 + slot], bd_s.at[n], bd_r.at[n], down)
+    def climb_own(c):
+        return remote(x_ref.at[c, p], blk.at[2, c], bu_s.at[c], bu_r.at[c], up)
+
+    def descend_own():
+        return remote(x_ref.at[:, p], blk.at[3 + p], bd_s.at[0], bd_r.at[0], down)
+
+    def descend_other():
+        return remote(blk.at[1 - p], blk.at[4 - p], bd_s.at[1], bd_r.at[1], down)
+
+    def load(n, f, slot):
+        return pltpu.make_async_copy(x_ref.at[:, f], blk.at[slot], in_s.at[n])
 
     def core_copy(k):
         return remote(cs.at[k], cr.at[k], c_s.at[k], c_r.at[k], twin)
@@ -66,6 +76,8 @@
     def energy_copy(s, d):
         return remote(es.at[s], er.at[s, d - 1], e_s.at[s, d - 1], e_r.at[s, d - 1], win_peer(d))
 
+    load(0, p, p).start()
+    load(1, 1 - p, 5).start()
     barrier = pltpu.get_barrier_semaphore()
 
     def greet(*others):
@@ -81,16 +93,15 @@
 
     for c in range(2):
         exchange(c).start()
-    blk[p] = x_ref[:, p]
 
     @pl.when(has_down)
     def _():
-        descend(p, 0).start()
+        descend_own().start()
 
     @pl.when(jnp.logical_and(has_up, odd))
     def _():
         for c in range(2):
-            climb(c).start()
+            climb_own(c).start()
 
     def energy(s):
         def step(i, total):
@@ -114,7 +125,7 @@
         lane = lax.broadcasted_iota(jnp.int32, (rows, width), 1)
         wide = jnp.broadcast_to(scale[s, 0:1], (rows, width))
         picked = jnp.sum(jnp.where(row == lane, wide, 0.0), axis=1, keepdims=True)
-        column[kb] = jnp.broadcast_to(picked * (1.0 / (LIFT * windows)), (rows, 128))
+        column[kb] = jnp.broadcast_to(picked * (1.0 / LIFT), (rows, 128))
 
     def build_left(kb, s):
         lift = jnp.asarray(LIFT, jnp.bfloat16)
@@ -152,7 +163,7 @@
         for c in range(2):
             for tile in range(width // 128):
                 at = pl.ds(((r * 2 + c) * (width // 128) + tile) * 2 + f, rows, stride=step_rows)
-                out_ref[at, :] = value[c, :, tile * 128:(tile + 1) * 128]
+                flat[at, :] = value[c, :, tile * 128:(tile + 1) * 128]
 
     def total_of(m, kb, s):
         cut = pl.ds(pl.multiple_of(y * 2 * rows, 2 * rows), 2 * rows)
@@ -208,9 +219,10 @@
         each(product, g)
         each(fold, g)
 
+    load(0, p, p).wait()
     build_left(p, p)
     each(product, "mine")
-    blk[5] = x_ref[:, 1 - p]
+    load(1, 1 - p, 5).wait()
     build_left(4, 5)
     each(product, "twist")
     each(fold, "mine")
@@ -220,14 +232,14 @@
     for c in range(2):
         exchanged(c).wait_recv()
         pl.when(jnp.logical_and(has_up, even))(lambda: climb(c).start())
-    pl.when(has_down)(lambda: descend(1 - p, 1).start())
+    pl.when(has_down)(lambda: descend_other().start())
     build_left(1 - p, 1 - p)
     make("pair")
     energy(1 - p)
 
     @pl.when(has_up)
     def _():
-        descend(p, 0).wait_recv()
+        descend_own().wait_recv()
         build_left(2 + p, 3 + p)
         make("above")
         energy(3 + p)
@@ -255,7 +267,7 @@
         finish_energy(3 + p)
         finish_column(2 + p, 3 + p)
         each(final_up, "above")
-        descend(1 - p, 1).wait_recv()
+        descend_other().wait_recv()
         build_left(3 - p, 4 - p)
         make("other")
         energy(4 - p)
@@ -267,13 +279,18 @@
         finish_energy(2)
         each(final_here, "below")
 
+    pl.when(jnp.logical_and(has_both, even))(lambda: each(final_up, "span"))
+
     @pl.when(has_up)
     def _():
         finish_energy(4 - p)
         finish_column(3 - p, 4 - p)
         each(final_up, "other")
 
-    pl.when(has_both)(lambda: each(final_up, "span"))
+    pl.when(jnp.logical_and(has_both, odd))(lambda: each(final_up, "span"))
+
+    def written(r):
+        return pltpu.make_async_copy(out_ref.at[:, r], result_ref.at[:, r], out_s.at[r])
 
     def receive(r, carry):
         @pl.when(jnp.logical_and(chan >= r, r >= 1))
@@ -291,6 +308,7 @@
             for f in range(2):
                 store(r, f, jnp.zeros((2, rows, width), jnp.float32))
 
+        written(r).start()
         return carry
 
     lax.fori_loop(0, 4, receive, 0)
@@ -305,8 +323,8 @@
 
     @pl.when(has_down)
     def _():
-        descend(p, 0).wait_send()
-        descend(1 - p, 1).wait_send()
+        descend_own().wait_send()
+        descend_other().wait_send()
 
     def sent(m, kb, s, q, r):
         core_copy(m).wait_send()
@@ -345,6 +363,8 @@
         energy_sent(4)
 
     pl.when(has_both)(lambda: each(sent_up, "span"))
+    for r in range(rounds):
+        written(r).wait()
 
 
 def on_device(n_chan, n_win, spectra, near):
@@ -352,13 +372,15 @@
     rounds = near.shape[1] + 1
     rows, n_y = width // n_win, n_win // 2
     bf, f32 = jnp.bfloat16, jnp.float32
+    out_shape = (rows, rounds, 2 * freqs * (width // 128), 128)
     dma = pltpu.SemaphoreType.DMA
     out = pl.pallas_call(
         functools.partial(kernel, n_chan, n_win, float(depth * n_win)),
-        out_shape=jax.ShapeDtypeStruct((rows * rounds * 2 * freqs * (width // 128), 128), f32),
-        in_specs=[pl.BlockSpec(memory_space=pltpu.VMEM), pl.BlockSpec(memory_space=pltpu.SMEM)],
-        out_specs=pl.BlockSpec(memory_space=pltpu.VMEM),
+        out_shape=jax.ShapeDtypeStruct(out_shape, f32),
+        in_specs=[pl.BlockSpec(memory_space=pl.ANY), pl.BlockSpec(memory_space=pltpu.SMEM)],
+        out_specs=pl.BlockSpec(memory_space=pl.ANY),
         scratch_shapes=[
+            pltpu.VMEM(out_shape, f32),
             pltpu.VMEM((6, 2, depth, width), bf),
             pltpu.VMEM((5, 2 * width, 2 * depth), bf),
             pltpu.VMEM((8, width, width), f32),
@@ -374,14 +396,14 @@
             pltpu.VMEM((5, rows, 128), f32),
             dma((2,)), dma((2,)), dma((2,)), dma((2,)), dma((2,)), dma((2,)), dma((8,)), dma((8,)),
             dma((8, n_y - 1)), dma((8, n_y - 1)), dma((8,)), dma((rounds, 2)),
-            dma((6, n_win - 1)), dma((6, n_win - 1)),
+            dma((6, n_win - 1)), dma((6, n_win - 1)), dma((2,)), dma((rounds,)),
         ],
         compiler_params=pltpu.CompilerParams(
             collective_id=0, has_side_effects=True, vmem_limit_bytes=56 * 1024 * 1024),
         cost_estimate=pl.CostEstimate(
             flops=64 * depth * width * width, bytes_accessed=6 * 1024 * 1024, transcendentals=0),
     )(spectra, near)
-    out = out.reshape(rows, rounds, 2, width // 128, freqs, 128)
+    out = (out * (1.0 / (depth * n_win))).reshape(rows, rounds, 2, width // 128, freqs, 128)
     return jnp.transpose(out, (0, 1, 2, 4, 3, 5)).reshape(rows, rounds, 2, freqs, width)
 
 

time: 92.8 us -> 84.6 us (0.912)
  local copies, waits for them, and re-layouts: 7.34 us -> 0 us
  Pallas kernels: 85.3 us -> 79.4 us
  other arithmetic: 0 us -> 5.04 us
    unnamed x1 -> x0, local copies, waits for them, and re-layouts: 7.34 us -> none
    pallas_call x1, Pallas kernels: 85.3 us -> 79.4 us  [on_device(): pl.pallas_call(functools.partial(kernel, n_chan, n_win, float(depth * n_w...]
    mul x0 -> x1, other arithmetic: none -> 5.04 us  [on_device(): out * (1.0 / (depth * n_win))]
where the time goes in v4:
time: 84.6 us; the launch traced here: 84.4 us
  Pallas kernels  79.4 us (94%)
  other arithmetic  5.04 us (6%)
    pallas_call x1, Pallas kernels, on_device(): pl.pallas_call(functools.partial(kernel, n_chan, n_win, float(depth * n_w...  79.4 us
    mul x1, other arithmetic, on_device(): out * (1.0 / (depth * n_win))  5.04 us

profile of v4, /device:TPU:16, one launch (start us, length us, event | category | flops | bytes accessed | tf_op | source)
XLA Modules:
  0.0 84.4 jit_solution(15465914864273422006)
XLA Ops:
  0.0 79.4 %shard_map.28 = f32[128,4,16,128]{3,2,1,0:T(8,128)} custom-call(bf16[2,2,512,512]{3,2,1,0:T(8,128)(2,1)} %x_ref.1, s32[1,3]{1,0:T(1,128)} %near_ref.1), custom_call_target="tpu_custom_call" | custom-call | flops 8589934592 | bytes 6291456 | tf_op jit(solution)/shard_map/pallas_call | solution.py:377
  79.4 5.0 %broadcast_multiply_fusion = f32[128,4,16,128]{3,2,1,0:T(8,128)} fusion(f32[128,4,16,128]{3,2,1,0:T(8,128)} %shard_map.28), kind=kLoop, calls=%fused_computation | loop fusion | flops 1048576 | bytes 8388608 | tf_op jit(solution)/shard_map/mul | solution.py:406

commit v5 on v4

--- a/solution.py
+++ b/solution.py
@@ -109,7 +109,7 @@
             return total + jnp.sum((part * part).reshape(2 * 8, 8, width), axis=0)
 
         total = lax.fori_loop(0, depth // 64, step, jnp.zeros((8, width), jnp.float32))
-        es[s] = jnp.broadcast_to(jnp.sum(total, axis=0, keepdims=True), (8, width))
+        es[s] = jnp.sum(total, axis=0, keepdims=True)
         for d in range(1, n_win):
             energy_copy(s, d).start()
 
@@ -118,7 +118,7 @@
         for d in range(1, n_win):
             energy_copy(s, d).wait_recv()
             total = total + er[s, d - 1]
-        scale[s] = lax.rsqrt(total / windows + EPS)
+        scale[s] = jnp.broadcast_to(lax.rsqrt(total / windows + EPS), (8, width))
 
     def finish_column(kb, s):
         row = lax.broadcasted_iota(jnp.int32, (rows, width), 0) + win * rows
@@ -390,8 +390,8 @@
             pltpu.VMEM((8, n_y - 1, 2 * rows, width), bf),
             pltpu.VMEM((8, 2, rows, width), bf),
             pltpu.VMEM((rounds, 2, 2, rows, width), bf),
-            pltpu.VMEM((6, 8, width), f32),
-            pltpu.VMEM((6, n_win - 1, 8, width), f32),
+            pltpu.VMEM((6, 1, width), f32),
+            pltpu.VMEM((6, n_win - 1, 1, width), f32),
             pltpu.VMEM((6, 8, width), f32),
             pltpu.VMEM((5, rows, 128), f32),
             dma((2,)), dma((2,)), dma((2,)), dma((2,)), dma((2,)), dma((2,)), dma((8,)), dma((8,)),

time: 84.6 us -> 83.7 us (0.989)
  Pallas kernels: 79.4 us -> 78.5 us
    pallas_call x1, Pallas kernels: 79.4 us -> 78.5 us  [on_device(): pl.pallas_call(functools.partial(kernel, n_chan, n_win, float(depth * n_w...]
where the time goes in v5:
time: 83.7 us; the launch traced here: 83.5 us
  Pallas kernels  78.5 us (94%)
  other arithmetic  5.04 us (6%)
    pallas_call x1, Pallas kernels, on_device(): pl.pallas_call(functools.partial(kernel, n_chan, n_win, float(depth * n_w...  78.5 us
    mul x1, other arithmetic, on_device(): out * (1.0 / (depth * n_win))  5.04 us

profile of v5, /device:TPU:16, one launch (start us, length us, event | category | flops | bytes accessed | tf_op | source)
XLA Modules:
  0.0 83.5 jit_solution(2156554028621148278)
XLA Ops:
  0.0 78.5 %shard_map.28 = f32[128,4,16,128]{3,2,1,0:T(8,128)} custom-call(bf16[2,2,512,512]{3,2,1,0:T(8,128)(2,1)} %x_ref.1, s32[1,3]{1,0:T(1,128)} %near_ref.1), custom_call_target="tpu_custom_call" | custom-call | flops 8589934592 | bytes 6291456 | tf_op jit(solution)/shard_map/pallas_call | solution.py:377
  78.5 5.0 %broadcast_multiply_fusion = f32[128,4,16,128]{3,2,1,0:T(8,128)} fusion(f32[128,4,16,128]{3,2,1,0:T(8,128)} %shard_map.28), kind=kLoop, calls=%fused_computation | loop fusion | flops 1048576 | bytes 8388608 | tf_op jit(solution)/shard_map/mul | solution.py:406
